TPU v7x, 32 devices: a whole 2x2x4 slice. The times are simulated.
32 devices in a mesh: grp: 2 (over x), row: 16 (over z, y, core).
Axes of the slice: x: 2, y: 2, z: 4, core: 2. Of those that a mesh axis runs over, the one named last changes fastest.
Arguments:
- matrix: bfloat16 [32, 2048, 16384], P(('grp', 'row')), parts along dimension 0, may hold values from -1 to 1
- probes: bfloat16 [16384, 128], P(('grp', 'row')), parts along dimension 0, may hold values from -6 to 6
Outputs:
- basis_out: bfloat16 [16384, 128], P(('grp', 'row')), parts along dimension 0
- sketch_out: bfloat16 [32, 4096, 128], P(('grp', 'row')), parts along dimension 0
There are 2 independent parts, one for each index of `grp`. A program takes and returns all parts, laid end to end along the dimension named above; each array names one. Nothing has to cross between parts.
All inputs are finite; a program needn't handle non-finite values.
Results may differ from a plain program's by a relative error of at most 0.012.
Values may be sent and summed in bfloat16 or wider, within the bound.
A program may use at most 192 MiB of HBM per device.

v0:
```python
import math
import jax
import jax.numpy as jnp
from jax import lax
from jax.sharding import PartitionSpec as P

GRID_ROWS = 4
ITERS = 2


def from_partner(shard, axis, bit):
    return lax.ppermute(shard, axis, [(i, i ^ 1 << bit) for i in range(lax.axis_size(axis))])


def orthonormal(product, gram_matrix, rescale):
    factor = jnp.linalg.cholesky(gram_matrix)
    solved = lax.linalg.triangular_solve(
        factor, product, left_side=False, lower=True, transpose_a=True
    )
    return (solved * rescale).astype(jnp.bfloat16)


def digit_set(device, level):
    return device // 2**level % 2 == 1


def per_device(matrix, probes):
    tile_block = matrix[0]
    tile_rows = tile_block.shape[0]
    grid_cols = lax.axis_size("row") // GRID_ROWS
    col_levels = grid_cols.bit_length() - 1
    row_levels = GRID_ROWS.bit_length() - 1
    device = lax.axis_index("row")
    rescale = math.sqrt(GRID_ROWS * tile_rows)
    current = probes
    sketch_block = None
    for iteration in range(ITERS):
        panel = current
        for level in range(col_levels):
            other = from_partner(panel, "row", level)
            panel = jnp.where(
                digit_set(device, level),
                jnp.concatenate([other, panel], 0),
                jnp.concatenate([panel, other], 0),
            )
        partial_value = lax.dot_general(
            tile_block, panel, (((0,), (0,)), ((), ())), preferred_element_type=jnp.float32
        )
        for level in range(row_levels):
            partial_value = partial_value + from_partner(
                partial_value.astype(jnp.bfloat16), "row", col_levels + level
            ).astype(partial_value.dtype)
        sketch = partial_value.astype(jnp.bfloat16)
        share_rows = sketch.shape[0] // GRID_ROWS
        grid_row = device // grid_cols
        sketch_block = lax.dynamic_slice_in_dim(sketch, grid_row * share_rows, share_rows, 0)
        image = jnp.dot(tile_block, sketch, preferred_element_type=jnp.float32)
        for level in reversed(range(col_levels)):
            half_rows = image.shape[0] // 2
            lower_part = image[:half_rows]
            upper_part = image[half_rows:]
            upward = digit_set(device, level)
            sent = jnp.where(upward, lower_part, upper_part)
            kept = jnp.where(upward, upper_part, lower_part)
            image = kept + from_partner(sent.astype(jnp.bfloat16), "row", level).astype(sent.dtype)
        local_gram = jnp.dot(
            image.T, image, precision=lax.Precision.HIGHEST, preferred_element_type=jnp.float32
        )
        gram_matrix = lax.psum(local_gram, "row")
        current = orthonormal(image, gram_matrix, rescale)
    return (current, sketch_block[None])


def solution(mesh):
    placed = (P(("grp", "row"), None, None), P(("grp", "row"), None))
    return jax.shard_map(
        per_device,
        mesh=mesh,
        in_specs=placed,
        out_specs=(P(("grp", "row"), None), P(("grp", "row"), None, None)),
        check_vma=False,
    )
```

profile of v0, /device:TPU:8, one launch (start us, length us, event | category | flops | bytes accessed | tf_op | source)
XLA Modules:
  0.0 968.9 jit_solution(17788045940890955766)
XLA Ops:
  7.2 0.0 all-reduce.3.cloned.1.call-start
  7.2 1.0 copy.12
  8.2 0.1 collective-permute-start
  8.3 1.3 collective-permute-done
  9.6 0.1 maximum_select_fusion.4
  9.7 1.6 collective-permute-start.1
  11.3 6.8 collective-permute-done.1
  18.2 28.6 %fusion.50 = (bf16[16384,128]{0,1:T(8,128)(2,1)}, f32[16384,128]{0,1:T(8,128)}) fusion(bf16[1,2048,16384]{2,1,0:T(8,128)(2,1)} %param.5, bf16[1024,128]{0,1:T(8,128)(2,1)S(1)} %maximum_select_fusion.4, bf16[1024,128]{0,1:T(8,128)(2,1)S(1)} %collective-permute-done.1, pred[]{:T(512)S(6)} %eq.22), kind=kOutput, calls=%fused_computation.70 | convolution fusion | flops 8594391040 | bytes 80216064 | tf_op jit(solution)/shard_map/dot_general | solution.py:46
  46.7 0.2 collective-permute-start.2
  47.0 91.8 %collective-permute-done.2 = bf16[16384,128]{0,1:T(8,128)(2,1)S(1)} collective-permute-done((bf16[16384,128]{0,1:T(8,128)(2,1)}, bf16[16384,128]{0,1:T(8,128)(2,1)S(1)}, u32[]{:S(2)}, u32[]{:S(2)}) %collective-permute-start.2) | collective-permute-done | bytes 4194336 | tf_op jit(solution)/shard_map/ppermute | solution.py:12
  138.8 5.7 fusion.14
  144.5 0.0 copy-done
  144.5 2.7 collective-permute-start.3
  147.1 178.2 %collective-permute-done.3 = bf16[16384,128]{0,1:T(8,128)(2,1)} collective-permute-done((bf16[16384,128]{0,1:T(8,128)(2,1)S(1)}, bf16[16384,128]{0,1:T(8,128)(2,1)}, u32[]{:S(2)}, u32[]{:S(2)}) %collective-permute-start.3) | collective-permute-done | bytes 4194336 | tf_op jit(solution)/shard_map/ppermute | solution.py:12
  325.3 33.8 %fusion.16 = f32[2048,128]{0,1:T(8,128)S(1)} fusion(bf16[1,2048,16384]{2,1,0:T(8,128)(2,1)} %param.5, bf16[16384,128]{0,1:T(8,128)(2,1)} %collective-permute-done.3, f32[16384,128]{0,1:T(8,128)} %get-tuple-element.9, bf16[16384,128]{0,1:T(8,128)(2,1)} %copy-done), kind=kOutput, calls=%fused_computation.16 | convolution fusion | flops 8600420352 | bytes 84934656 | tf_op jit(solution)/shard_map/dot_general | solution.py:57
  359.1 0.1 select_convert_fusion.1
  359.2 1.6 collective-permute-start.4
  360.8 6.7 collective-permute-done.4
  367.5 0.1 convert_add_fusion.3
  367.6 0.1 collective-permute-start.5
  367.7 1.3 collective-permute-done.5
  369.0 1.0 fusion.46
  370.1 0.0 all-reduce.3.cloned.1.call-update
  370.1 0.2 all-reduce.5.cloned.1.call-start
  370.3 89.0 %all-reduce.3.cloned.1.call-done = f32[128,128]{0,1:T(8,128)} async-done(((f32[128,128]{0,1:T(8,128)}), f32[128,128]{0,1:T(8,128)}) %all-reduce.3.cloned.1.call-update) | async-done | bytes 65552 | tf_op jit(solution)/shard_map/psum | solution.py:69
  459.3 0.9 copy.16
  460.3 0.9 fusion.43
  461.1 11.7 %cholesky.44 = f32[128,128]{1,0:T(8,128)S(1)} custom-call(f32[128,128]{1,0:T(8,128)S(1)} %fusion.43), custom_call_target="Cholesky" | custom-call | tf_op jit(solution)/shard_map/jit(cholesky)/cholesky | solution.py:16
  472.9 0.6 compare_reduce_fusion.1
  473.5 0.7 fusion.38
  474.2 9.8 %custom-call.6 = f32[1,128,128]{1,2,0:T(8,128)S(1)} custom-call(f32[1,128,128]{2,1,0:T(8,128)S(1)} %fusion.38), custom_call_target="InvertDiagBlocksLowerTriangular" | custom-call | tf_op jit(solution)/shard_map/triangular_solve/custom-call.0 | solution.py:17
  484.0 0.4 fusion.24
  484.4 0.1 collective-permute-start.6
  484.5 1.3 collective-permute-done.6
  485.8 0.1 maximum_select_fusion.5
  485.9 0.6 collective-permute-start.7
  486.6 7.8 collective-permute-done.7
  494.4 28.6 %fusion.51 = (bf16[16384,128]{0,1:T(8,128)(2,1)}, f32[16384,128]{0,1:T(8,128)}) fusion(bf16[1,2048,16384]{2,1,0:T(8,128)(2,1)} %param.5, bf16[1024,128]{0,1:T(8,128)(2,1)S(1)} %maximum_select_fusion.5, bf16[1024,128]{0,1:T(8,128)(2,1)S(1)} %collective-permute-done.7, pred[]{:T(512)S(6)} %eq.22), kind=kOutput, calls=%fused_computation.71 | convolution fusion | flops 8594391040 | bytes 80216064 | tf_op jit(solution)/shard_map/dot_general | solution.py:46
  523.0 0.0 collective-permute-start.8
  523.0 92.0 %collective-permute-done.8 = bf16[16384,128]{0,1:T(8,128)(2,1)S(1)} collective-permute-done((bf16[16384,128]{0,1:T(8,128)(2,1)}, bf16[16384,128]{0,1:T(8,128)(2,1)S(1)}, u32[]{:S(2)}, u32[]{:S(2)}) %collective-permute-start.8) | collective-permute-done | bytes 4194336 | tf_op jit(solution)/shard_map/ppermute | solution.py:12
  615.0 4.4 fusion.15
  619.4 1.5 collective-permute-start.9
  620.9 178.3 %collective-permute-done.9 = bf16[16384,128]{0,1:T(8,128)(2,1)} collective-permute-done((bf16[16384,128]{0,1:T(8,128)(2,1)S(1)}, bf16[16384,128]{0,1:T(8,128)(2,1)}, u32[]{:S(2)}, u32[]{:S(2)}) %collective-permute-start.9) | collective-permute-done | bytes 4194336 | tf_op jit(solution)/shard_map/ppermute | solution.py:12
  799.2 8.2 add_convert_fusion
  807.4 29.7 %fusion.19 = f32[2048,128]{0,1:T(8,128)S(1)} fusion(bf16[16384,128]{0,1:T(8,128)(2,1)} %add_convert_fusion, bf16[1,2048,16384]{2,1,0:T(8,128)(2,1)} %param.5), kind=kOutput, calls=%fused_computation.17 | convolution fusion | flops 8589934592 | bytes 72351744 | tf_op jit(solution)/shard_map/dot_general | solution.py:57
  837.1 0.1 select_convert_fusion
  837.1 0.5 collective-permute-start.10
  837.6 7.8 collective-permute-done.10
  845.4 0.1 convert_add_fusion.2
  845.5 0.1 collective-permute-start.11
  845.6 1.3 collective-permute-done.11
  846.9 1.0 fusion.47
  848.0 0.0 all-reduce.5.cloned.1.call-update
  848.0 1.3 constant_dynamic-slice_fusion
  849.3 1.3 copy.19
  850.6 85.7 %all-reduce.5.cloned.1.call-done = f32[128,128]{0,1:T(8,128)} async-done(((f32[128,128]{0,1:T(8,128)}), f32[128,128]{0,1:T(8,128)}) %all-reduce.5.cloned.1.call-update) | async-done | bytes 65552 | tf_op jit(solution)/shard_map/psum | solution.py:69
  936.3 0.9 copy.18
  937.2 0.9 fusion.41
  938.0 11.7 %cholesky.55 = f32[128,128]{1,0:T(8,128)S(1)} custom-call(f32[128,128]{1,0:T(8,128)S(1)} %fusion.41), custom_call_target="Cholesky" | custom-call | tf_op jit(solution)/shard_map/jit(cholesky)/cholesky | solution.py:16
  949.8 0.6 compare_reduce_fusion
  950.4 0.7 fusion.39
  951.1 9.8 %custom-call.7 = f32[1,128,128]{1,2,0:T(8,128)S(1)} custom-call(f32[1,128,128]{2,1,0:T(8,128)S(1)} %fusion.39), custom_call_target="InvertDiagBlocksLowerTriangular" | custom-call | tf_op jit(solution)/shard_map/triangular_solve/custom-call.0 | solution.py:17
  960.9 0.4 fusion.25
  961.3 0.8 copy.20
  (5 shorter events, 0.1 us)
Async XLA Ops:
  7.2 452.2 %all-reduce.3.cloned.1.call-start = ((), (), s32[]{:S(2)}) async-start(), calls=%async_computation | async-start | bytes 131072 | tf_op jit(solution)/shard_map/psum | solution.py:69
  8.2 1.4 collective-permute-start
  9.7 8.4 collective-permute-start.1
  46.7 92.0 %collective-permute-start.2 = (bf16[16384,128]{0,1:T(8,128)(2,1)}, bf16[16384,128]{0,1:T(8,128)(2,1)S(1)}, u32[]{:S(2)}, u32[]{:S(2)}) collective-permute-start(bf16[16384,128]{0,1:T(8,128)(2,1)} %get-tuple-element.8), channel_id=1, source_target_pairs={{0,4},{1,5},{2,6},{3,7},{4,0},{5,1},{6,2},{7,3},{8,12},{9,13},{10,... | collective-permute-start | bytes 12582920 | tf_op jit(solution)/shard_map/ppermute | solution.py:12
  138.8 5.7 copy-start
  144.5 180.8 %collective-permute-start.3 = (bf16[16384,128]{0,1:T(8,128)(2,1)S(1)}, bf16[16384,128]{0,1:T(8,128)(2,1)}, u32[]{:S(2)}, u32[]{:S(2)}) collective-permute-start(bf16[16384,128]{0,1:T(8,128)(2,1)S(1)} %fusion.14), channel_id=1, source_target_pairs={{0,8},{1,9},{2,10},{3,11},{4,12},{5,13},{6,14},{7,15},{8,0},{9,1},... | collective-permute-start | bytes 12582920 | tf_op jit(solution)/shard_map/ppermute | solution.py:12
  359.2 8.3 collective-permute-start.4
  367.6 1.4 collective-permute-start.5
  370.1 566.2 %all-reduce.5.cloned.1.call-start = ((), (), s32[]{:S(2)}) async-start(), calls=%async_computation.1 | async-start | bytes 131072 | tf_op jit(solution)/shard_map/psum | solution.py:69
  484.4 1.4 collective-permute-start.6
  485.9 8.4 collective-permute-start.7
  523.0 92.0 %collective-permute-start.8 = (bf16[16384,128]{0,1:T(8,128)(2,1)}, bf16[16384,128]{0,1:T(8,128)(2,1)S(1)}, u32[]{:S(2)}, u32[]{:S(2)}) collective-permute-start(bf16[16384,128]{0,1:T(8,128)(2,1)} %get-tuple-element.10), channel_id=1, source_target_pairs={{0,4},{1,5},{2,6},{3,7},{4,0},{5,1},{6,2},{7,3},{8,12},{9,13},{10,... | collective-permute-start | bytes 12582920 | tf_op jit(solution)/shard_map/ppermute | solution.py:12
  619.4 179.8 %collective-permute-start.9 = (bf16[16384,128]{0,1:T(8,128)(2,1)S(1)}, bf16[16384,128]{0,1:T(8,128)(2,1)}, u32[]{:S(2)}, u32[]{:S(2)}) collective-permute-start(bf16[16384,128]{0,1:T(8,128)(2,1)S(1)} %fusion.15), channel_id=1, source_target_pairs={{0,8},{1,9},{2,10},{3,11},{4,12},{5,13},{6,14},{7,15},{8,0},{9,1},... | collective-permute-start | bytes 12582920 | tf_op jit(solution)/shard_map/ppermute | solution.py:12
  837.1 8.3 collective-permute-start.10
  845.5 1.4 collective-permute-start.11
Sparse Core Ops, SparseCore 0:
  370.2 89.0 all-reduce.2
  848.1 88.1 all-reduce.4
where the time goes:
time: 970 us; the launch traced here: 969 us
  waiting for transfers between devices  749 us (77%)
  matrix products  124 us (13%)
  other arithmetic  66.2 us (7%)
  between operations  14.3 us (1%)
    ppermute x12, waiting for transfers between devices, from_partner(): lax.ppermute(shard, axis, [(i, i ^ 1 << bit) for i in range(lax.axis_size...  575 us
    psum x2, waiting for transfers between devices, per_device(): gram_matrix = lax.psum(local_gram, 'row')  175 us
    dot_general x2, matrix products, per_device(): image = jnp.dot(tile_block, sketch, preferred_element_type=jnp.float32)  63.5 us
    dot_general x2, matrix products, per_device(): lax.dot_general(tile_block, panel, (((0,), (0,)), ((), ())), preferred_el...  57.2 us
    another operation x6, other arithmetic, orthonormal(): factor = jnp.linalg.cholesky(gram_matrix)  24.8 us
    another operation x4, other arithmetic, orthonormal(): lax.linalg.triangular_solve(factor, product, left_side=False, lower=True,...  20.9 us
  transfers between devices with their start and end apart: 14, of which 14 were waited for; matrix products, arithmetic and copies ran while one was open for 0% of the time, Pallas kernels for 0%

commit v1 on v0

--- a/solution.py
+++ b/solution.py
@@ -66,7 +66,11 @@
         local_gram = jnp.dot(
             image.T, image, precision=lax.Precision.HIGHEST, preferred_element_type=jnp.float32
         )
-        gram_matrix = lax.psum(local_gram, "row")
+        gram_matrix = local_gram
+        for hop in (1, 2, 4, 8):
+            gram_matrix = gram_matrix + lax.ppermute(
+                gram_matrix, "row", [(dev, dev ^ hop) for dev in range(16)]
+            )
         current = orthonormal(image, gram_matrix, rescale)
     return (current, sketch_block[None])
 

time: 970 us -> 809 us (0.83)
  waiting for transfers between devices: 749 us -> 589 us
  starting transfers between devices: 9.21 us -> 25.9 us
  between operations: 14.3 us -> 0.93 us
    psum x2 -> x0, waiting for transfers between devices: 175 us -> none  [per_device(): gram_matrix = lax.psum(local_gram, 'row')]
    ppermute x0 -> x8, waiting for transfers between devices: none -> 16.7 us  [per_device(): lax.ppermute(gram_matrix, 'row', [(dev, dev ^ hop) for dev in range(16)])]
    ppermute x0 -> x8, starting transfers between devices: none -> 12.6 us  [per_device(): lax.ppermute(gram_matrix, 'row', [(dev, dev ^ hop) for dev in range(16)])]
  transfers between devices with their start and end apart: 14 -> 20, of which waited for: 14 -> 19; matrix products, arithmetic and copies ran while one was open for 0% -> 0% of each run, Pallas kernels for 0% -> 0%
where the time goes in v1:
time: 809 us; the launch traced here: 807 us
  waiting for transfers between devices  589 us (73%)
  matrix products  122 us (15%)
  other arithmetic  64.6 us (8%)
  starting transfers between devices  25.9 us (3%)
    ppermute x12, waiting for transfers between devices, from_partner(): lax.ppermute(shard, axis, [(i, i ^ 1 << bit) for i in range(lax.axis_size...  572 us
    dot_general x2, matrix products, per_device(): image = jnp.dot(tile_block, sketch, preferred_element_type=jnp.float32)  63.7 us
    dot_general x2, matrix products, per_device(): lax.dot_general(tile_block, panel, (((0,), (0,)), ((), ())), preferred_el...  57.1 us
    another operation x6, other arithmetic, orthonormal(): factor = jnp.linalg.cholesky(gram_matrix)  24.8 us
    another operation x4, other arithmetic, orthonormal(): lax.linalg.triangular_solve(factor, product, left_side=False, lower=True,...  20.9 us
    ppermute x8, waiting for transfers between devices, per_device(): lax.ppermute(gram_matrix, 'row', [(dev, dev ^ hop) for dev in range(16)])  16.7 us
  transfers between devices with their start and end apart: 20, of which 19 were waited for; matrix products, arithmetic and copies ran while one was open for 0% of the time, Pallas kernels for 0%

profile of v1, /device:TPU:8, one launch (start us, length us, event | category | flops | bytes accessed | tf_op | source)
XLA Modules:
  0.0 807.0 jit_solution(16915393175166134201)
XLA Ops:
  0.6 1.0 copy.14
  1.7 1.3 collective-permute-done
  3.1 0.1 maximum_select_fusion.4
  3.1 1.6 collective-permute-start.1
  4.7 6.8 collective-permute-done.1
  11.6 28.5 %fusion.50 = (bf16[16384,128]{0,1:T(8,128)(2,1)}, f32[16384,128]{0,1:T(8,128)}) fusion(bf16[1,2048,16384]{2,1,0:T(8,128)(2,1)} %param.5, bf16[1024,128]{0,1:T(8,128)(2,1)S(1)} %maximum_select_fusion.4, bf16[1024,128]{0,1:T(8,128)(2,1)S(1)} %collective-permute-done.1, pred[]{:T(512)S(6)} %eq.22), kind=kOutput, calls=%fused_computation.70 | convolution fusion | flops 8594391040 | bytes 80216064 | tf_op jit(solution)/shard_map/dot_general | solution.py:46
  40.1 0.2 collective-permute-start.2
  40.3 91.8 %collective-permute-done.2 = bf16[16384,128]{0,1:T(8,128)(2,1)S(1)} collective-permute-done((bf16[16384,128]{0,1:T(8,128)(2,1)}, bf16[16384,128]{0,1:T(8,128)(2,1)S(1)}, u32[]{:S(2)}, u32[]{:S(2)}) %collective-permute-start.2) | collective-permute-done | bytes 4194336 | tf_op jit(solution)/shard_map/ppermute | solution.py:12
  132.1 5.7 fusion.14
  137.9 2.7 collective-permute-start.3
  140.5 178.2 %collective-permute-done.3 = bf16[16384,128]{0,1:T(8,128)(2,1)} collective-permute-done((bf16[16384,128]{0,1:T(8,128)(2,1)S(1)}, bf16[16384,128]{0,1:T(8,128)(2,1)}, u32[]{:S(2)}, u32[]{:S(2)}) %collective-permute-start.3) | collective-permute-done | bytes 4194336 | tf_op jit(solution)/shard_map/ppermute | solution.py:12
  318.7 34.0 %fusion.16 = f32[2048,128]{0,1:T(8,128)S(1)} fusion(bf16[1,2048,16384]{2,1,0:T(8,128)(2,1)} %param.5, bf16[16384,128]{0,1:T(8,128)(2,1)} %collective-permute-done.3, f32[16384,128]{0,1:T(8,128)} %get-tuple-element.9, bf16[16384,128]{0,1:T(8,128)(2,1)} %copy-done), kind=kOutput, calls=%fused_computation.16 | convolution fusion | flops 8600420352 | bytes 84934656 | tf_op jit(solution)/shard_map/dot_general | solution.py:57
  352.7 1.6 collective-permute-start.4
  354.3 6.7 collective-permute-done.4
  361.0 0.1 convert_add_fusion.3
  361.2 1.3 collective-permute-done.5
  362.6 0.4 fusion.46
  363.0 0.2 collective-permute-start.6
  363.2 1.1 collective-permute-done.6
  364.3 1.6 collective-permute-start.7
  365.9 2.7 collective-permute-done.7
  368.7 1.3 collective-permute-start.8
  370.0 3.0 collective-permute-done.8
  373.0 3.5 collective-permute-start.9
  376.6 2.2 collective-permute-done.9
  378.8 0.1 copy.19
  378.9 11.7 %cholesky.44 = f32[128,128]{1,0:T(8,128)S(1)} custom-call(f32[128,128]{1,0:T(8,128)S(1)} %fusion.43), custom_call_target="Cholesky" | custom-call | tf_op jit(solution)/shard_map/jit(cholesky)/cholesky | solution.py:16
  390.7 0.6 compare_reduce_fusion.1
  391.3 0.7 fusion.38
  392.0 9.8 %custom-call.6 = f32[1,128,128]{1,2,0:T(8,128)S(1)} custom-call(f32[1,128,128]{2,1,0:T(8,128)S(1)} %fusion.38), custom_call_target="InvertDiagBlocksLowerTriangular" | custom-call | tf_op jit(solution)/shard_map/triangular_solve/custom-call.0 | solution.py:17
  401.8 0.4 fusion.24
  402.3 1.3 collective-permute-done.10
  403.6 0.1 maximum_select_fusion.5
  403.7 1.6 collective-permute-start.11
  405.3 6.8 collective-permute-done.11
  412.2 28.5 %fusion.51 = (bf16[16384,128]{0,1:T(8,128)(2,1)}, f32[16384,128]{0,1:T(8,128)}) fusion(bf16[1,2048,16384]{2,1,0:T(8,128)(2,1)} %param.5, bf16[1024,128]{0,1:T(8,128)(2,1)S(1)} %maximum_select_fusion.5, bf16[1024,128]{0,1:T(8,128)(2,1)S(1)} %collective-permute-done.11, pred[]{:T(512)S(6)} %eq.22), kind=kOutput, calls=%fused_computation.71 | convolution fusion | flops 8594391040 | bytes 80216064 | tf_op jit(solution)/shard_map/dot_general | solution.py:46
  440.7 0.7 collective-permute-start.12
  441.4 91.3 %collective-permute-done.12 = bf16[16384,128]{0,1:T(8,128)(2,1)S(1)} collective-permute-done((bf16[16384,128]{0,1:T(8,128)(2,1)}, bf16[16384,128]{0,1:T(8,128)(2,1)S(1)}, u32[]{:S(2)}, u32[]{:S(2)}) %collective-permute-start.12) | collective-permute-done | bytes 4194336 | tf_op jit(solution)/shard_map/ppermute | solution.py:12
  532.7 4.4 fusion.15
  537.1 3.1 collective-permute-start.13
  540.3 178.3 %collective-permute-done.13 = bf16[16384,128]{0,1:T(8,128)(2,1)} collective-permute-done((bf16[16384,128]{0,1:T(8,128)(2,1)S(1)}, bf16[16384,128]{0,1:T(8,128)(2,1)}, u32[]{:S(2)}, u32[]{:S(2)}) %collective-permute-start.13) | collective-permute-done | bytes 4194336 | tf_op jit(solution)/shard_map/ppermute | solution.py:12
  718.5 8.2 %add_convert_fusion = bf16[16384,128]{0,1:T(8,128)(2,1)} fusion(bf16[16384,128]{0,1:T(8,128)(2,1)} %collective-permute-done.13, f32[16384,128]{0,1:T(8,128)} %get-tuple-element.11, bf16[16384,128]{0,1:T(8,128)(2,1)S(1)} %collective-permute-done.12), kind=kLoop, calls=%fused_computation.10 | loop fusion | flops 10485760 | bytes 20971520 | tf_op jit(solution)/shard_map/convert_element_type | solution.py:53
  726.7 29.7 %fusion.19 = f32[2048,128]{0,1:T(8,128)S(1)} fusion(bf16[16384,128]{0,1:T(8,128)(2,1)} %add_convert_fusion, bf16[1,2048,16384]{2,1,0:T(8,128)(2,1)} %param.5), kind=kOutput, calls=%fused_computation.17 | convolution fusion | flops 8589934592 | bytes 72351744 | tf_op jit(solution)/shard_map/dot_general | solution.py:57
  756.5 1.6 collective-permute-start.14
  758.0 6.7 collective-permute-done.14
  764.7 0.1 convert_add_fusion.2
  764.9 1.3 collective-permute-done.15
  766.3 0.4 fusion.47
  766.7 0.2 collective-permute-start.16
  766.9 1.1 collective-permute-done.16
  768.0 1.6 collective-permute-start.17
  769.6 2.7 collective-permute-done.17
  772.4 0.6 collective-permute-start.18
  772.9 3.8 collective-permute-done.18
  776.7 3.6 collective-permute-start.19
  780.2 1.3 constant_dynamic-slice_fusion
  781.5 1.3 copy.23
  782.9 0.1 copy.22
  783.0 11.7 %cholesky.55 = f32[128,128]{1,0:T(8,128)S(1)} custom-call(f32[128,128]{1,0:T(8,128)S(1)} %fusion.41), custom_call_target="Cholesky" | custom-call | tf_op jit(solution)/shard_map/jit(cholesky)/cholesky | solution.py:16
  794.7 0.6 compare_reduce_fusion
  795.4 0.7 fusion.39
  796.0 9.8 %custom-call.7 = f32[1,128,128]{1,2,0:T(8,128)S(1)} custom-call(f32[1,128,128]{2,1,0:T(8,128)S(1)} %fusion.39), custom_call_target="InvertDiagBlocksLowerTriangular" | custom-call | tf_op jit(solution)/shard_map/triangular_solve/custom-call.0 | solution.py:17
  805.9 0.4 fusion.25
  806.3 0.8 copy.24
  (23 shorter events, 0.6 us)
Async XLA Ops:
  1.6 1.4 collective-permute-start
  3.1 8.4 %collective-permute-start.1 = (bf16[1024,128]{0,1:T(8,128)(2,1)S(1)}, bf16[1024,128]{0,1:T(8,128)(2,1)S(1)}, u32[]{:S(2)}, u32[]{:S(2)}) collective-permute-start(bf16[1024,128]{0,1:T(8,128)(2,1)S(1)} %maximum_select_fusion.4), channel_id=1, source_target_pairs={{0,2},{1,3},{2,0},{3,1},{4,6},{5,7},{6,4},{7,5},{8,10},{9,11},{10,... | collective-permute-start | bytes 786440 | tf_op jit(solution)/shard_map/ppermute | solution.py:12
  40.1 92.0 %collective-permute-start.2 = (bf16[16384,128]{0,1:T(8,128)(2,1)}, bf16[16384,128]{0,1:T(8,128)(2,1)S(1)}, u32[]{:S(2)}, u32[]{:S(2)}) collective-permute-start(bf16[16384,128]{0,1:T(8,128)(2,1)} %get-tuple-element.8), channel_id=1, source_target_pairs={{0,4},{1,5},{2,6},{3,7},{4,0},{5,1},{6,2},{7,3},{8,12},{9,13},{10,... | collective-permute-start | bytes 12582920 | tf_op jit(solution)/shard_map/ppermute | solution.py:12
  132.1 5.7 copy-start
  137.9 180.8 %collective-permute-start.3 = (bf16[16384,128]{0,1:T(8,128)(2,1)S(1)}, bf16[16384,128]{0,1:T(8,128)(2,1)}, u32[]{:S(2)}, u32[]{:S(2)}) collective-permute-start(bf16[16384,128]{0,1:T(8,128)(2,1)S(1)} %fusion.14), channel_id=1, source_target_pairs={{0,8},{1,9},{2,10},{3,11},{4,12},{5,13},{6,14},{7,15},{8,0},{9,1},... | collective-permute-start | bytes 12582920 | tf_op jit(solution)/shard_map/ppermute | solution.py:12
  352.7 8.3 %collective-permute-start.4 = (bf16[1024,128]{0,1:T(8,128)(2,1)S(1)}, bf16[1024,128]{0,1:T(8,128)(2,1)S(1)}, u32[]{:S(2)}, u32[]{:S(2)}) collective-permute-start(bf16[1024,128]{0,1:T(8,128)(2,1)S(1)} %select_convert_fusion.1), channel_id=1, source_target_pairs={{0,2},{1,3},{2,0},{3,1},{4,6},{5,7},{6,4},{7,5},{8,10},{9,11},{10,... | collective-permute-start | bytes 786440 | tf_op jit(solution)/shard_map/ppermute | solution.py:12
  361.2 1.4 collective-permute-start.5
  363.0 1.3 collective-permute-start.6
  364.3 4.3 collective-permute-start.7
  368.7 4.3 collective-permute-start.8
  373.0 5.8 collective-permute-start.9
  402.2 1.4 collective-permute-start.10
  403.7 8.4 %collective-permute-start.11 = (bf16[1024,128]{0,1:T(8,128)(2,1)S(1)}, bf16[1024,128]{0,1:T(8,128)(2,1)S(1)}, u32[]{:S(2)}, u32[]{:S(2)}) collective-permute-start(bf16[1024,128]{0,1:T(8,128)(2,1)S(1)} %maximum_select_fusion.5), channel_id=1, source_target_pairs={{0,2},{1,3},{2,0},{3,1},{4,6},{5,7},{6,4},{7,5},{8,10},{9,11},{10,... | collective-permute-start | bytes 786440 | tf_op jit(solution)/shard_map/ppermute | solution.py:12
  440.7 92.0 %collective-permute-start.12 = (bf16[16384,128]{0,1:T(8,128)(2,1)}, bf16[16384,128]{0,1:T(8,128)(2,1)S(1)}, u32[]{:S(2)}, u32[]{:S(2)}) collective-permute-start(bf16[16384,128]{0,1:T(8,128)(2,1)} %get-tuple-element.10), channel_id=1, source_target_pairs={{0,4},{1,5},{2,6},{3,7},{4,0},{5,1},{6,2},{7,3},{8,12},{9,13},{10,... | collective-permute-start | bytes 12582920 | tf_op jit(solution)/shard_map/ppermute | solution.py:12
  537.1 181.4 %collective-permute-start.13 = (bf16[16384,128]{0,1:T(8,128)(2,1)S(1)}, bf16[16384,128]{0,1:T(8,128)(2,1)}, u32[]{:S(2)}, u32[]{:S(2)}) collective-permute-start(bf16[16384,128]{0,1:T(8,128)(2,1)S(1)} %fusion.15), channel_id=1, source_target_pairs={{0,8},{1,9},{2,10},{3,11},{4,12},{5,13},{6,14},{7,15},{8,0},{9,1},... | collective-permute-start | bytes 12582920 | tf_op jit(solution)/shard_map/ppermute | solution.py:12
  756.5 8.3 %collective-permute-start.14 = (bf16[1024,128]{0,1:T(8,128)(2,1)S(1)}, bf16[1024,128]{0,1:T(8,128)(2,1)S(1)}, u32[]{:S(2)}, u32[]{:S(2)}) collective-permute-start(bf16[1024,128]{0,1:T(8,128)(2,1)S(1)} %select_convert_fusion), channel_id=1, source_target_pairs={{0,2},{1,3},{2,0},{3,1},{4,6},{5,7},{6,4},{7,5},{8,10},{9,11},{10,... | collective-permute-start | bytes 786440 | tf_op jit(solution)/shard_map/ppermute | solution.py:12
  764.9 1.4 collective-permute-start.15
  766.7 1.3 collective-permute-start.16
  768.0 4.3 collective-permute-start.17
  772.4 4.3 collective-permute-start.18
  776.7 6.2 collective-permute-start.19
